TPU v7x, 32 devices: a whole 2x2x4 slice. The times are simulated.
32 devices in a mesh: gx: 4 (over z), gy: 2 (over y), gz: 4 (over x, core).
Axes of the slice: x: 2, y: 2, z: 4, core: 2. Of those that a mesh axis runs over, the one named last changes fastest.
Arguments:
- density: float32 [64, 16, 1024], P('gx', 'gy', 'gz'), may hold values from 0.05 to 0.95
- voxel_kind: int32 [64, 16, 1024], P('gx', 'gy', 'gz'), may hold values from 0 to 15, as said below
Outputs:
- new_density: float32 [64, 16, 1024], P('gx', 'gy', 'gz')
- velocity: float32 [64, 16, 1024], P('gx', 'gy', 'gz')
- adjoint: float32 [64, 16, 1024], P('gx', 'gy', 'gz')
Inputs may be any that keep to these rules, and one draw needn't show every extreme that they name: `voxel_kind`: 0 to 12 mark design voxels, 13 solid, 14 inlet, 15 outlet.
All inputs are finite; a program needn't handle non-finite values.
Results may differ from a plain program's by a relative error of at most 0.0003.
Values sent between devices are 32-bit elements; how exact they have to be, the bound alone decides.
A program may use at most 128 MiB of HBM per device.

v0:
```python
import jax
import jax.numpy as jnp
from jax import lax
from jax.sharding import PartitionSpec as P

RADIUS = 6
LEVELS = 3
CYCLES = 2
COARSE_SWEEPS = 4
BISECT = 9
penalty_solid = 0.2
penalty_fluid = 0.001
convexity = 0.1
damping = 0.8
step_size = 0.1
move_limit = 0.2
volume_fraction = 0.45
epsilon = 1e-06


def with_halo(cells, sides, width):
    for axis, dim in sides:
        count = lax.axis_size(axis)
        ends = count - 1
        head = lax.slice_in_dim(cells, 0, width, axis=dim)
        tail = lax.slice_in_dim(cells, cells.shape[dim] - width, cells.shape[dim], axis=dim)
        cells = jnp.concatenate(
            [
                lax.ppermute(tail, axis, [(i, (i + 1) % count) for i in range(ends)]),
                cells,
                lax.ppermute(head, axis, [((i + 1) % count, i) for i in range(ends)]),
            ],
            axis=dim,
        )
    return cells


def smooth_axis(padded, axis_dim, length):
    result = None
    for offset in range(-RADIUS, RADIUS + 1):
        tap_term = float(RADIUS + 1 - abs(offset)) * lax.slice_in_dim(
            padded, RADIUS + offset, RADIUS + offset + length, axis=axis_dim
        )
        result = tap_term if result is None else result + tap_term
    return result


def spread(field_values):
    padded = with_halo(field_values, (("gx", 0),), RADIUS)
    field_values = smooth_axis(padded, 0, field_values.shape[0])
    padded = with_halo(field_values, (("gy", 1),), RADIUS)
    field_values = smooth_axis(padded, 1, field_values.shape[1])
    padded = with_halo(field_values, (("gz", 2),), RADIUS)
    return smooth_axis(padded, 2, field_values.shape[2])


def edge_sums(cell_count, first_index, grid_total):
    positions = first_index + jnp.arange(cell_count, dtype=jnp.int32)
    result = jnp.zeros((cell_count,), jnp.float32)
    for offset in range(-RADIUS, RADIUS + 1):
        moved = positions + offset
        inside = (moved >= 0) & (moved < grid_total)
        result = result + jnp.where(inside, float(RADIUS + 1 - abs(offset)), 0.0).astype(
            jnp.float32
        )
    return result


def neighbour_total(padded):
    beside = padded[..., 2:, 1:-1, 1:-1] + padded[..., :-2, 1:-1, 1:-1]
    beside = beside + padded[..., 1:-1, 2:, 1:-1] + padded[..., 1:-1, :-2, 1:-1]
    beside = beside + padded[..., 1:-1, 1:-1, 2:] + padded[..., 1:-1, 1:-1, :-2]
    return beside


def operate(field_values, brinkman_penalty, grid_scale):
    padded = with_halo(field_values, (("gx", 1), ("gy", 2), ("gz", 3)), 1)
    beside = neighbour_total(padded)
    return (6.0 * field_values - beside) * grid_scale + brinkman_penalty * field_values


def relax(field_values, forcing_term, brinkman_penalty, grid_scale, start_blank):
    diagonal = 6.0 * grid_scale + brinkman_penalty
    if start_blank:
        return damping * forcing_term / diagonal
    return (
        field_values
        + damping * (forcing_term - operate(field_values, brinkman_penalty, grid_scale)) / diagonal
    )


def restrict_grid(field_values):
    shape_a, shape_b, shape_c = field_values.shape[-3:]
    blocks = field_values.reshape(
        field_values.shape[:-3] + (shape_a // 2, 2, shape_b // 2, 2, shape_c // 2, 2)
    )
    return jnp.mean(blocks, axis=(-5, -3, -1))


def refine(field_values):
    return jnp.repeat(jnp.repeat(jnp.repeat(field_values, 2, axis=-3), 2, axis=-2), 2, axis=-1)


def multilevel_pass(
    field_values, forcing_term, penalty_pyramid, mesh_depth, start_blank, finest_penalty
):
    grid_scale = 0.25**mesh_depth
    brinkman_penalty = penalty_pyramid[mesh_depth]
    if mesh_depth == LEVELS - 1:
        field_values = relax(None, forcing_term, brinkman_penalty, grid_scale, True)
        for sweep_index in range(COARSE_SWEEPS - 1):
            field_values = relax(field_values, forcing_term, brinkman_penalty, grid_scale, False)
        return field_values
    field_values = relax(field_values, forcing_term, brinkman_penalty, grid_scale, start_blank)
    equation_misfit = forcing_term - operate(field_values, brinkman_penalty, grid_scale)
    coarse_update = multilevel_pass(
        None, restrict_grid(equation_misfit), penalty_pyramid, mesh_depth + 1, True, finest_penalty
    )
    field_values = field_values + refine(coarse_update)
    return relax(field_values, forcing_term, brinkman_penalty, grid_scale, False)


def compute_velocity(forcing_term, penalty_pyramid):
    field_values = None
    for vcycle_counter in range(CYCLES):
        field_values = multilevel_pass(
            field_values, forcing_term, penalty_pyramid, 0, vcycle_counter == 0, None
        )
    return field_values


def global_sums(partials):
    return lax.psum(partials, ("gx", "gy", "gz"))


def body(density, voxel_kind):
    size_x, size_y, size_z = density.shape
    total_x = size_x * lax.axis_size("gx")
    total_y = size_y * lax.axis_size("gy")
    total_z = size_z * lax.axis_size("gz")
    design = voxel_kind < 13
    solid_mask = voxel_kind == 13
    inflow_mask = voxel_kind == 14
    outflow_face = voxel_kind == 15
    sums_x = edge_sums(size_x, lax.axis_index("gx") * size_x, total_x)
    sums_y = edge_sums(size_y, lax.axis_index("gy") * size_y, total_y)
    sums_z = edge_sums(size_z, lax.axis_index("gz") * size_z, total_z)
    normal = sums_x[:, None, None] * sums_y[None, :, None] * sums_z[None, None, :]
    filtered = spread(density) / normal
    interp = penalty_solid + (penalty_fluid - penalty_solid) * filtered * (1.0 + convexity) / (
        filtered + convexity
    )
    brinkman_penalty = jnp.where(
        design, interp, jnp.where(solid_mask, penalty_solid, penalty_fluid)
    )
    penalty_pyramid = [brinkman_penalty]
    for mesh_depth in range(LEVELS - 1):
        penalty_pyramid.append(restrict_grid(penalty_pyramid[-1]))
    inflow_forcing = inflow_mask.astype(jnp.float32)
    outflow_forcing = outflow_face.astype(jnp.float32)
    velocity = compute_velocity(inflow_forcing[None], penalty_pyramid)[0]
    adjoint = compute_velocity(outflow_forcing[None], penalty_pyramid)[0]
    slope = (
        (penalty_fluid - penalty_solid)
        * (1.0 + convexity)
        * convexity
        / ((filtered + convexity) * (filtered + convexity))
    )
    gradient = jnp.where(design, adjoint * velocity * slope, 0.0)
    sensitivity = spread(gradient / normal)
    global_stats = global_sums(
        jnp.stack([jnp.sum(sensitivity * sensitivity), jnp.sum(design.astype(jnp.float32))])
    )
    cell_total = float(total_x * total_y * total_z)
    scaled = sensitivity / jnp.sqrt(global_stats[0] / cell_total + epsilon)
    target = volume_fraction * global_stats[1]
    trial_base = density - step_size * scaled
    lower_bound = jnp.maximum(0.0, density - move_limit)
    upper_bound = jnp.minimum(1.0, density + move_limit)

    def local_volume(candidate):
        return jnp.sum(
            jnp.where(design, jnp.clip(trial_base + candidate, lower_bound, upper_bound), 0.0)
        )

    start_bounds = (jnp.float32(-2.0), jnp.float32(2.0))

    def halve(step_index, bounds):
        low_end, high_end = bounds
        middle = (low_end + high_end) * 0.5
        volume = global_sums(local_volume(middle)[None])[0]
        above_target = volume > target
        return (jnp.where(above_target, low_end, middle), jnp.where(above_target, middle, high_end))

    low_end, high_end = lax.fori_loop(0, BISECT, halve, start_bounds)
    multiplier = (low_end + high_end) * 0.5
    new_density = jnp.where(
        design, jnp.clip(trial_base + multiplier, lower_bound, upper_bound), density
    )
    return (new_density, velocity, adjoint)


def solution(mesh):
    return jax.shard_map(
        body,
        mesh=mesh,
        in_specs=(P("gx", "gy", "gz"), P("gx", "gy", "gz")),
        out_specs=(P("gx", "gy", "gz"), P("gx", "gy", "gz"), P("gx", "gy", "gz")),
        check_vma=False,
    )
```

profile of v0, /device:TPU:0, one launch (start us, length us, event | category | flops | bytes accessed | tf_op | source)
XLA Modules:
  0.0 1169.2 jit_solution(6395994082612991756)
XLA Ops:
  1.5 4.9 collective-permute-start
  51.8 9.7 reshape.1089
  66.5 9.7 reshape.1088
  81.6 4.8 collective-permute-start.13
  121.3 5.4 collective-permute-done.22
  203.6 9.7 reshape.1093
  256.0 5.6 collective-permute-done.112
  364.9 6.6 collective-permute-start.137
  417.5 9.7 reshape.1091
  452.8 5.6 collective-permute-start.143
  557.6 9.7 reshape.1095
  610.0 5.6 collective-permute-done.160
  718.6 4.8 collective-permute-start.186
  742.6 47.2 %psum.14 = f32[2]{0:T(128)S(1)} all-reduce(f32[2]{0:T(128)S(1)} %pad_maximum_fusion.538), channel_id=1, replica_groups=mesh['gx'=4,'gy'=2,'gz'=4] {'gx','gy','gz'}, use_global_device_ids=true, to_apply=%region_12.13 | all-reduce | flops 2 | bytes 16 | tf_op jit(solution)/shard_map/psum | solution.py:133
  791.8 376.6 %while.12 = (s32[]{:T(128)}, f32[]{:T(128)}, f32[]{:T(128)}, f32[16,8,256]{2,1,0:T(8,128)S(1)}, f32[16,8,256]{2,1,0:T(8,128)S(1)}, /*index=5*/f32[16,8,256]{2,1,...) while((s32[]{:T(128)}, f32[]{:T(128)}, f32[]{:T(128)}, ...), condition=%wide.region_16.17_spmd, body=%wide.region_13.16_spmd.sunk | while | flops 163847 | bytes 426160 | solution.py:195
  792.5 40.4 %psum.16 = f32[]{:T(128)} all-reduce(f32[]{:T(128)} %select_reduce_fusion.2), channel_id=1, replica_groups=mesh['gx'=4,'gy'=2,'gz'=4] {'gx','gy','gz'}, use_global_device_ids=true, to_apply=%region_15.15 | all-reduce | flops 1 | bytes 8 | tf_op jit(solution)/shard_map/while/body/eval_jaxpr/psum | solution.py:133
  834.2 40.3 %psum.16 = f32[]{:T(128)} all-reduce(f32[]{:T(128)} %select_reduce_fusion.2), channel_id=1, replica_groups=mesh['gx'=4,'gy'=2,'gz'=4] {'gx','gy','gz'}, use_global_device_ids=true, to_apply=%region_15.15 | all-reduce | flops 1 | bytes 8 | tf_op jit(solution)/shard_map/while/body/eval_jaxpr/psum | solution.py:133
  875.9 40.7 %psum.16 = f32[]{:T(128)} all-reduce(f32[]{:T(128)} %select_reduce_fusion.2), channel_id=1, replica_groups=mesh['gx'=4,'gy'=2,'gz'=4] {'gx','gy','gz'}, use_global_device_ids=true, to_apply=%region_15.15 | all-reduce | flops 1 | bytes 8 | tf_op jit(solution)/shard_map/while/body/eval_jaxpr/psum | solution.py:133
  917.9 40.2 %psum.16 = f32[]{:T(128)} all-reduce(f32[]{:T(128)} %select_reduce_fusion.2), channel_id=1, replica_groups=mesh['gx'=4,'gy'=2,'gz'=4] {'gx','gy','gz'}, use_global_device_ids=true, to_apply=%region_15.15 | all-reduce | flops 1 | bytes 8 | tf_op jit(solution)/shard_map/while/body/eval_jaxpr/psum | solution.py:133
  959.6 40.8 %psum.16 = f32[]{:T(128)} all-reduce(f32[]{:T(128)} %select_reduce_fusion.2), channel_id=1, replica_groups=mesh['gx'=4,'gy'=2,'gz'=4] {'gx','gy','gz'}, use_global_device_ids=true, to_apply=%region_15.15 | all-reduce | flops 1 | bytes 8 | tf_op jit(solution)/shard_map/while/body/eval_jaxpr/psum | solution.py:133
  1001.7 40.2 %psum.16 = f32[]{:T(128)} all-reduce(f32[]{:T(128)} %select_reduce_fusion.2), channel_id=1, replica_groups=mesh['gx'=4,'gy'=2,'gz'=4] {'gx','gy','gz'}, use_global_device_ids=true, to_apply=%region_15.15 | all-reduce | flops 1 | bytes 8 | tf_op jit(solution)/shard_map/while/body/eval_jaxpr/psum | solution.py:133
  1043.2 40.8 %psum.16 = f32[]{:T(128)} all-reduce(f32[]{:T(128)} %select_reduce_fusion.2), channel_id=1, replica_groups=mesh['gx'=4,'gy'=2,'gz'=4] {'gx','gy','gz'}, use_global_device_ids=true, to_apply=%region_15.15 | all-reduce | flops 1 | bytes 8 | tf_op jit(solution)/shard_map/while/body/eval_jaxpr/psum | solution.py:133
  1085.4 40.2 %psum.16 = f32[]{:T(128)} all-reduce(f32[]{:T(128)} %select_reduce_fusion.2), channel_id=1, replica_groups=mesh['gx'=4,'gy'=2,'gz'=4] {'gx','gy','gz'}, use_global_device_ids=true, to_apply=%region_15.15 | all-reduce | flops 1 | bytes 8 | tf_op jit(solution)/shard_map/while/body/eval_jaxpr/psum | solution.py:133
  1126.9 40.8 %psum.16 = f32[]{:T(128)} all-reduce(f32[]{:T(128)} %select_reduce_fusion.2), channel_id=1, replica_groups=mesh['gx'=4,'gy'=2,'gz'=4] {'gx','gy','gz'}, use_global_device_ids=true, to_apply=%region_15.15 | all-reduce | flops 1 | bytes 8 | tf_op jit(solution)/shard_map/while/body/eval_jaxpr/psum | solution.py:133
  (705 shorter events, 653.8 us)
Async XLA Ops:
  47.5 18.1 %collective-permute-start.10 = (f32[1,18,10,1]{3,0,2,1:T(1,128)S(1)}, f32[1,18,10,1]{3,0,2,1:T(1,128)S(1)}, u32[]{:S(2)}, u32[]{:S(2)}) collective-permute-start(f32[1,18,10,1]{3,0,2,1:T(1,128)S(1)} %get-tuple-element.139), channel_id=1, source_target_pairs={{1,0},{2,1},{3,2},{5,4},{6,5},{7,6},{9,8},{10,9},{11,10},{13,12},{... | collective-permute-start | bytes 2168 | tf_op jit(solution)/shard_map/ppermute | solution.py:31
  48.8 16.8 %collective-permute-start.11 = (f32[1,18,10,1]{3,0,2,1:T(1,128)S(1)}, f32[1,18,10,1]{3,0,2,1:T(1,128)S(1)}, u32[]{:S(2)}, u32[]{:S(2)}) collective-permute-start(f32[1,18,10,1]{3,0,2,1:T(1,128)S(1)} %get-tuple-element.140), channel_id=1, source_target_pairs={{0,1},{1,2},{2,3},{4,5},{5,6},{6,7},{8,9},{9,10},{10,11},{12,13},{... | collective-permute-start | bytes 2168 | tf_op jit(solution)/shard_map/ppermute | solution.py:29
  126.8 12.0 %collective-permute-start.24 = (f32[1,1,2,64]{3,1,2,0:T(1,128)S(1)}, f32[1,1,2,64]{3,1,2,0:T(1,128)S(1)}, u32[]{:S(2)}, u32[]{:S(2)}) collective-permute-start(f32[1,1,2,64]{3,1,2,0:T(1,128)S(1)} %get-tuple-element.344), channel_id=1, source_target_pairs={{8,0},{16,8},{24,16},{9,1},{17,9},{25,17},{10,2},{18,10},{26,18},{... | collective-permute-start | bytes 1544 | tf_op jit(solution)/shard_map/ppermute | solution.py:31
  179.4 12.2 %collective-permute-start.36 = (f32[1,1,4,128]{3,2,1,0:T(4,128)S(1)}, f32[1,1,4,128]{3,2,1,0:T(4,128)S(1)}, u32[]{:S(2)}, u32[]{:S(2)}) collective-permute-start(f32[1,1,4,128]{3,2,1,0:T(4,128)S(1)} %get-tuple-element.282), channel_id=1, source_target_pairs={{8,0},{16,8},{24,16},{9,1},{17,9},{25,17},{10,2},{18,10},{26,18},{... | collective-permute-start | bytes 6152 | tf_op jit(solution)/shard_map/ppermute | solution.py:31
  198.9 18.4 %collective-permute-start.40 = (f32[1,10,6,1]{3,0,2,1:T(1,128)S(1)}, f32[1,10,6,1]{3,0,2,1:T(1,128)S(1)}, u32[]{:S(2)}, u32[]{:S(2)}) collective-permute-start(f32[1,10,6,1]{3,0,2,1:T(1,128)S(1)} %get-tuple-element.229), channel_id=1, source_target_pairs={{1,0},{2,1},{3,2},{5,4},{6,5},{7,6},{9,8},{10,9},{11,10},{13,12},{... | collective-permute-start | bytes 728 | tf_op jit(solution)/shard_map/ppermute | solution.py:31
  200.2 17.1 %collective-permute-start.41 = (f32[1,10,6,1]{3,0,2,1:T(1,128)S(1)}, f32[1,10,6,1]{3,0,2,1:T(1,128)S(1)}, u32[]{:S(2)}, u32[]{:S(2)}) collective-permute-start(f32[1,10,6,1]{3,0,2,1:T(1,128)S(1)} %get-tuple-element.230), channel_id=1, source_target_pairs={{0,1},{1,2},{2,3},{4,5},{5,6},{6,7},{8,9},{9,10},{10,11},{12,13},{... | collective-permute-start | bytes 728 | tf_op jit(solution)/shard_map/ppermute | solution.py:29
  326.6 12.0 %collective-permute-start.42 = (f32[1,1,8,256]{3,2,1,0:T(8,128)S(1)}, f32[1,1,8,256]{3,2,1,0:T(8,128)S(1)}, u32[]{:S(2)}, u32[]{:S(2)}) collective-permute-start(f32[1,1,8,256]{3,2,1,0:T(8,128)S(1)} %get-tuple-element.198), channel_id=1, source_target_pairs={{8,0},{16,8},{24,16},{9,1},{17,9},{25,17},{10,2},{18,10},{26,18},{... | collective-permute-start | bytes 24584 | tf_op jit(solution)/shard_map/ppermute | solution.py:31
  357.2 14.3 %collective-permute-start.48 = (f32[1,1,8,256]{3,2,1,0:T(8,128)S(1)}, f32[1,1,8,256]{3,2,1,0:T(8,128)S(1)}, u32[]{:S(2)}, u32[]{:S(2)}) collective-permute-start(f32[1,1,8,256]{3,2,1,0:T(8,128)S(1)} %get-tuple-element.196), channel_id=1, source_target_pairs={{8,0},{16,8},{24,16},{9,1},{17,9},{25,17},{10,2},{18,10},{26,18},{... | collective-permute-start | bytes 24584 | tf_op jit(solution)/shard_map/ppermute | solution.py:31
  358.5 13.0 %collective-permute-start.49 = (f32[1,1,8,256]{3,2,1,0:T(8,128)S(1)}, f32[1,1,8,256]{3,2,1,0:T(8,128)S(1)}, u32[]{:S(2)}, u32[]{:S(2)}) collective-permute-start(f32[1,1,8,256]{3,2,1,0:T(8,128)S(1)} %get-tuple-element.195), channel_id=1, source_target_pairs={{0,8},{8,16},{16,24},{1,9},{9,17},{17,25},{2,10},{10,18},{18,26},{... | collective-permute-start | bytes 24584 | tf_op jit(solution)/shard_map/ppermute | solution.py:29
  363.6 13.9 %collective-permute-start.136 = (f32[1,18,10,1]{3,0,2,1:T(1,128)S(1)}, f32[1,18,10,1]{3,0,2,1:T(1,128)S(1)}, u32[]{:S(2)}, u32[]{:S(2)}) collective-permute-start(f32[1,18,10,1]{3,0,2,1:T(1,128)S(1)} %get-tuple-element.155), channel_id=1, source_target_pairs={{1,0},{2,1},{3,2},{5,4},{6,5},{7,6},{9,8},{10,9},{11,10},{13,12},{... | collective-permute-start | bytes 2168 | tf_op jit(solution)/shard_map/ppermute | solution.py:31
  364.9 12.6 %collective-permute-start.137 = (f32[1,18,10,1]{3,0,2,1:T(1,128)S(1)}, f32[1,18,10,1]{3,0,2,1:T(1,128)S(1)}, u32[]{:S(2)}, u32[]{:S(2)}) collective-permute-start(f32[1,18,10,1]{3,0,2,1:T(1,128)S(1)} %get-tuple-element.156), channel_id=1, source_target_pairs={{0,1},{1,2},{2,3},{4,5},{5,6},{6,7},{8,9},{9,10},{10,11},{12,13},{... | collective-permute-start | bytes 2168 | tf_op jit(solution)/shard_map/ppermute | solution.py:29
  413.5 23.6 %collective-permute-start.141 = (f32[1,18,1,256]{3,2,1,0:T(1,128)S(1)}, f32[1,18,1,256]{3,2,1,0:T(1,128)S(1)}, u32[]{:S(2)}, u32[]{:S(2)}) collective-permute-start(f32[1,18,1,256]{3,2,1,0:T(1,128)S(1)} %get-tuple-element.176), channel_id=1, source_target_pairs={{0,4},{1,5},{2,6},{3,7},{8,12},{9,13},{10,14},{11,15},{16,20},{17,... | collective-permute-start | bytes 55304 | tf_op jit(solution)/shard_map/ppermute | solution.py:29
  415.3 21.8 %collective-permute-start.140 = (f32[1,18,1,256]{3,2,1,0:T(1,128)S(1)}, f32[1,18,1,256]{3,2,1,0:T(1,128)S(1)}, u32[]{:S(2)}, u32[]{:S(2)}) collective-permute-start(f32[1,18,1,256]{3,2,1,0:T(1,128)S(1)} %get-tuple-element.175), channel_id=1, source_target_pairs={{4,0},{5,1},{6,2},{7,3},{12,8},{13,9},{14,10},{15,11},{20,16},{21,... | collective-permute-start | bytes 55304 | tf_op jit(solution)/shard_map/ppermute | solution.py:31
  445.8 12.6 %collective-permute-start.64 = (f32[1,10,6,1]{3,0,2,1:T(1,128)S(1)}, f32[1,10,6,1]{3,0,2,1:T(1,128)S(1)}, u32[]{:S(2)}, u32[]{:S(2)}) collective-permute-start(f32[1,10,6,1]{3,0,2,1:T(1,128)S(1)} %get-tuple-element.225), channel_id=1, source_target_pairs={{1,0},{2,1},{3,2},{5,4},{6,5},{7,6},{9,8},{10,9},{11,10},{13,12},{... | collective-permute-start | bytes 728 | tf_op jit(solution)/shard_map/ppermute | solution.py:31
  451.5 14.5 %collective-permute-start.142 = (f32[1,18,10,1]{3,0,2,1:T(1,128)S(1)}, f32[1,18,10,1]{3,0,2,1:T(1,128)S(1)}, u32[]{:S(2)}, u32[]{:S(2)}) collective-permute-start(f32[1,18,10,1]{3,0,2,1:T(1,128)S(1)} %get-tuple-element.151), channel_id=1, source_target_pairs={{1,0},{2,1},{3,2},{5,4},{6,5},{7,6},{9,8},{10,9},{11,10},{13,12},{... | collective-permute-start | bytes 2168 | tf_op jit(solution)/shard_map/ppermute | solution.py:31
  452.8 13.2 %collective-permute-start.143 = (f32[1,18,10,1]{3,0,2,1:T(1,128)S(1)}, f32[1,18,10,1]{3,0,2,1:T(1,128)S(1)}, u32[]{:S(2)}, u32[]{:S(2)}) collective-permute-start(f32[1,18,10,1]{3,0,2,1:T(1,128)S(1)} %get-tuple-element.152), channel_id=1, source_target_pairs={{0,1},{1,2},{2,3},{4,5},{5,6},{6,7},{8,9},{9,10},{10,11},{12,13},{... | collective-permute-start | bytes 2168 | tf_op jit(solution)/shard_map/ppermute | solution.py:29
  480.8 12.0 %collective-permute-start.72 = (f32[1,1,2,64]{3,1,2,0:T(1,128)S(1)}, f32[1,1,2,64]{3,1,2,0:T(1,128)S(1)}, u32[]{:S(2)}, u32[]{:S(2)}) collective-permute-start(f32[1,1,2,64]{3,1,2,0:T(1,128)S(1)} %get-tuple-element.338), channel_id=1, source_target_pairs={{8,0},{16,8},{24,16},{9,1},{17,9},{25,17},{10,2},{18,10},{26,18},{... | collective-permute-start | bytes 1544 | tf_op jit(solution)/shard_map/ppermute | solution.py:31
  533.5 12.2 %collective-permute-start.84 = (f32[1,1,4,128]{3,2,1,0:T(4,128)S(1)}, f32[1,1,4,128]{3,2,1,0:T(4,128)S(1)}, u32[]{:S(2)}, u32[]{:S(2)}) collective-permute-start(f32[1,1,4,128]{3,2,1,0:T(4,128)S(1)} %get-tuple-element.270), channel_id=1, source_target_pairs={{8,0},{16,8},{24,16},{9,1},{17,9},{25,17},{10,2},{18,10},{26,18},{... | collective-permute-start | bytes 6152 | tf_op jit(solution)/shard_map/ppermute | solution.py:31
  553.0 18.4 %collective-permute-start.88 = (f32[1,10,6,1]{3,0,2,1:T(1,128)S(1)}, f32[1,10,6,1]{3,0,2,1:T(1,128)S(1)}, u32[]{:S(2)}, u32[]{:S(2)}) collective-permute-start(f32[1,10,6,1]{3,0,2,1:T(1,128)S(1)} %get-tuple-element.221), channel_id=1, source_target_pairs={{1,0},{2,1},{3,2},{5,4},{6,5},{7,6},{9,8},{10,9},{11,10},{13,12},{... | collective-permute-start | bytes 728 | tf_op jit(solution)/shard_map/ppermute | solution.py:31
  554.3 17.1 %collective-permute-start.89 = (f32[1,10,6,1]{3,0,2,1:T(1,128)S(1)}, f32[1,10,6,1]{3,0,2,1:T(1,128)S(1)}, u32[]{:S(2)}, u32[]{:S(2)}) collective-permute-start(f32[1,10,6,1]{3,0,2,1:T(1,128)S(1)} %get-tuple-element.222), channel_id=1, source_target_pairs={{0,1},{1,2},{2,3},{4,5},{5,6},{6,7},{8,9},{9,10},{10,11},{12,13},{... | collective-permute-start | bytes 728 | tf_op jit(solution)/shard_map/ppermute | solution.py:29
  644.8 12.0 %collective-permute-start.170 = (f32[1,6,1,64]{3,1,2,0:T(8,128)S(1)}, f32[1,6,1,64]{3,1,2,0:T(8,128)S(1)}, u32[]{:S(2)}, u32[]{:S(2)}) collective-permute-start(f32[1,6,1,64]{3,1,2,0:T(8,128)S(1)} %get-tuple-element.324), channel_id=1, source_target_pairs={{4,0},{5,1},{6,2},{7,3},{12,8},{13,9},{14,10},{15,11},{20,16},{21,... | collective-permute-start | bytes 4616 | tf_op jit(solution)/shard_map/ppermute | solution.py:31
  650.7 19.5 %collective-permute-start.90 = (f32[1,1,8,256]{3,2,1,0:T(8,128)S(1)}, f32[1,1,8,256]{3,2,1,0:T(8,128)S(1)}, u32[]{:S(2)}, u32[]{:S(2)}) collective-permute-start(f32[1,1,8,256]{3,2,1,0:T(8,128)S(1)} %get-tuple-element.192), channel_id=1, source_target_pairs={{8,0},{16,8},{24,16},{9,1},{17,9},{25,17},{10,2},{18,10},{26,18},{... | collective-permute-start | bytes 24584 | tf_op jit(solution)/shard_map/ppermute | solution.py:31
  652.0 18.2 %collective-permute-start.91 = (f32[1,1,8,256]{3,2,1,0:T(8,128)S(1)}, f32[1,1,8,256]{3,2,1,0:T(8,128)S(1)}, u32[]{:S(2)}, u32[]{:S(2)}) collective-permute-start(f32[1,1,8,256]{3,2,1,0:T(8,128)S(1)} %get-tuple-element.191), channel_id=1, source_target_pairs={{0,8},{8,16},{16,24},{1,9},{9,17},{17,25},{2,10},{10,18},{18,26},{... | collective-permute-start | bytes 24584 | tf_op jit(solution)/shard_map/ppermute | solution.py:29
  683.2 13.1 %collective-permute-start.92 = (f32[1,18,1,256]{3,2,1,0:T(1,128)S(1)}, f32[1,18,1,256]{3,2,1,0:T(1,128)S(1)}, u32[]{:S(2)}, u32[]{:S(2)}) collective-permute-start(f32[1,18,1,256]{3,2,1,0:T(1,128)S(1)} %get-tuple-element.162), channel_id=1, source_target_pairs={{4,0},{5,1},{6,2},{7,3},{12,8},{13,9},{14,10},{15,11},{20,16},{21,... | collective-permute-start | bytes 55304 | tf_op jit(solution)/shard_map/ppermute | solution.py:31
  (169 other events, 1272.9 us)
where the time goes:
time: 1180 us; the launch traced here: 1170 us
  starting transfers between devices  516 us (44%)
  blocking collectives  411 us (35%)
  waiting for transfers between devices  110 us (9%)
  local copies, waits for them, and re-layouts  66.6 us (6%)
  other arithmetic  52.5 us (4%)
    psum x10, blocking collectives, global_sums(): return lax.psum(partials, ('gx', 'gy', 'gz'))  411 us
    ppermute x96, starting transfers between devices, with_halo(): lax.ppermute(tail, axis, [(i, (i + 1) % count) for i in range(ends)])  392 us
    ppermute x96, starting transfers between devices, with_halo(): lax.ppermute(head, axis, [((i + 1) % count, i) for i in range(ends)])  125 us
    ppermute x96, waiting for transfers between devices, with_halo(): lax.ppermute(head, axis, [((i + 1) % count, i) for i in range(ends)])  59.9 us
    reshape x9, local copies, waits for them, and re-layouts, restrict_grid(): field_values.reshape(field_values.shape[:-3] + (shape_a // 2, 2, shape_b...  52.7 us
    ppermute x96, waiting for transfers between devices, with_halo(): lax.ppermute(tail, axis, [(i, (i + 1) % count) for i in range(ends)])  50.4 us
  transfers between devices with their start and end apart: 192, of which 64 were waited for; matrix products, arithmetic and copies ran while one was open for 6% of the time, Pallas kernels for 0%

commit v1 on v0

--- a/solution.py
+++ b/solution.py
@@ -130,7 +130,7 @@
 
 
 def global_sums(partials):
-    return lax.psum(partials, ("gx", "gy", "gz"))
+    return lax.psum(lax.psum(partials, ("gy", "gz")), "gx")
 
 
 def body(density, voxel_kind):

time: 1180 us -> 1000 us (0.85)
  blocking collectives: 411 us -> 231 us
    psum x10 -> x20, blocking collectives: 411 us -> 231 us  [global_sums(): return lax.psum(lax.psum(partials, ('gy', 'gz')), 'gx')]
  transfers between devices with their start and end apart: 192 -> 192, of which waited for: 64 -> 64; matrix products, arithmetic and copies ran while one was open for 6% -> 7% of each run, Pallas kernels for 0% -> 0%
where the time goes in v1:
time: 1000 us; the launch traced here: 988 us
  starting transfers between devices  516 us (52%)
  blocking collectives  231 us (23%)
  waiting for transfers between devices  110 us (11%)
  local copies, waits for them, and re-layouts  66.5 us (7%)
  other arithmetic  51.7 us (5%)
    ppermute x96, starting transfers between devices, with_halo(): lax.ppermute(tail, axis, [(i, (i + 1) % count) for i in range(ends)])  392 us
    psum x20, blocking collectives, global_sums(): return lax.psum(lax.psum(partials, ('gy', 'gz')), 'gx')  231 us
    ppermute x96, starting transfers between devices, with_halo(): lax.ppermute(head, axis, [((i + 1) % count, i) for i in range(ends)])  125 us
    ppermute x96, waiting for transfers between devices, with_halo(): lax.ppermute(head, axis, [((i + 1) % count, i) for i in range(ends)])  60 us
    reshape x9, local copies, waits for them, and re-layouts, restrict_grid(): field_values.reshape(field_values.shape[:-3] + (shape_a // 2, 2, shape_b...  52.6 us
    ppermute x96, waiting for transfers between devices, with_halo(): lax.ppermute(tail, axis, [(i, (i + 1) % count) for i in range(ends)])  50.4 us
    reduce_sum x10, other arithmetic, restrict_grid(): return jnp.mean(blocks, axis=(-5, -3, -1))  20.9 us
  transfers between devices with their start and end apart: 192, of which 64 were waited for; matrix products, arithmetic and copies ran while one was open for 7% of the time, Pallas kernels for 0%

profile of v1, /device:TPU:0, one launch (start us, length us, event | category | flops | bytes accessed | tf_op | source)
XLA Modules:
  0.0 987.6 jit_solution(3447951656686136035)
XLA Ops:
  51.8 9.7 reshape.1089
  66.5 9.7 reshape.1088
  203.6 9.7 reshape.1093
  417.5 9.7 reshape.1091
  557.6 9.7 reshape.1095
  742.4 17.4 %psum.28 = f32[2]{0:T(128)S(1)} all-reduce(f32[2]{0:T(128)S(1)} %pad_maximum_fusion.538), channel_id=1, replica_groups=mesh['gx'=4,'gy'=2,'gz'=4] {'gy','gz'}, use_global_device_ids=true, to_apply=%region_12.13 | all-reduce | flops 2 | bytes 16 | tf_op jit(solution)/shard_map/psum | solution.py:133
  759.8 13.6 %psum.29 = f32[2]{0:T(128)S(1)} all-reduce(f32[2]{0:T(128)S(1)} %psum.28), channel_id=1, replica_groups=mesh['gx'=4,'gy'=2,'gz'=4] {'gx'}, use_global_device_ids=true, to_apply=%region_13.14 | all-reduce | flops 2 | bytes 16 | tf_op jit(solution)/shard_map/psum | solution.py:133
  775.2 211.5 %while.12 = (s32[]{:T(128)}, f32[]{:T(128)}, f32[]{:T(128)}, f32[16,8,256]{2,1,0:T(8,128)S(1)}, f32[16,8,256]{2,1,0:T(8,128)S(1)}, /*index=5*/f32[16,8,256]{2,1,...) while((s32[]{:T(128)}, f32[]{:T(128)}, f32[]{:T(128)}, ...), condition=%wide.region_18.19_spmd, body=%wide.region_14.18_spmd.sunk | while | flops 163848 | bytes 426168 | solution.py:195
  775.8 12.4 %psum.32 = f32[1]{0:T(128)} all-reduce(f32[1]{0:T(128)} %bitcast.408), channel_id=1, replica_groups=mesh['gx'=4,'gy'=2,'gz'=4] {'gy','gz'}, use_global_device_ids=true, to_apply=%region_16.16 | all-reduce | flops 1 | bytes 8 | tf_op jit(solution)/shard_map/while/body/eval_jaxpr/psum | solution.py:133
  788.2 9.0 psum.33
  798.4 12.4 %psum.32 = f32[1]{0:T(128)} all-reduce(f32[1]{0:T(128)} %bitcast.408), channel_id=1, replica_groups=mesh['gx'=4,'gy'=2,'gz'=4] {'gy','gz'}, use_global_device_ids=true, to_apply=%region_16.16 | all-reduce | flops 1 | bytes 8 | tf_op jit(solution)/shard_map/while/body/eval_jaxpr/psum | solution.py:133
  810.8 11.0 %psum.33 = f32[]{:T(128)} all-reduce(f32[]{:T(128)} %bitcast.409), channel_id=1, replica_groups=mesh['gx'=4,'gy'=2,'gz'=4] {'gx'}, use_global_device_ids=true, to_apply=%region_17.17 | all-reduce | flops 1 | bytes 8 | tf_op jit(solution)/shard_map/while/body/eval_jaxpr/psum | solution.py:133
  823.1 12.4 %psum.32 = f32[1]{0:T(128)} all-reduce(f32[1]{0:T(128)} %bitcast.408), channel_id=1, replica_groups=mesh['gx'=4,'gy'=2,'gz'=4] {'gy','gz'}, use_global_device_ids=true, to_apply=%region_16.16 | all-reduce | flops 1 | bytes 8 | tf_op jit(solution)/shard_map/while/body/eval_jaxpr/psum | solution.py:133
  845.7 12.4 %psum.32 = f32[1]{0:T(128)} all-reduce(f32[1]{0:T(128)} %bitcast.408), channel_id=1, replica_groups=mesh['gx'=4,'gy'=2,'gz'=4] {'gy','gz'}, use_global_device_ids=true, to_apply=%region_16.16 | all-reduce | flops 1 | bytes 8 | tf_op jit(solution)/shard_map/while/body/eval_jaxpr/psum | solution.py:133
  858.1 11.0 %psum.33 = f32[]{:T(128)} all-reduce(f32[]{:T(128)} %bitcast.409), channel_id=1, replica_groups=mesh['gx'=4,'gy'=2,'gz'=4] {'gx'}, use_global_device_ids=true, to_apply=%region_17.17 | all-reduce | flops 1 | bytes 8 | tf_op jit(solution)/shard_map/while/body/eval_jaxpr/psum | solution.py:133
  870.3 12.4 %psum.32 = f32[1]{0:T(128)} all-reduce(f32[1]{0:T(128)} %bitcast.408), channel_id=1, replica_groups=mesh['gx'=4,'gy'=2,'gz'=4] {'gy','gz'}, use_global_device_ids=true, to_apply=%region_16.16 | all-reduce | flops 1 | bytes 8 | tf_op jit(solution)/shard_map/while/body/eval_jaxpr/psum | solution.py:133
  882.7 9.0 psum.33
  892.9 12.4 %psum.32 = f32[1]{0:T(128)} all-reduce(f32[1]{0:T(128)} %bitcast.408), channel_id=1, replica_groups=mesh['gx'=4,'gy'=2,'gz'=4] {'gy','gz'}, use_global_device_ids=true, to_apply=%region_16.16 | all-reduce | flops 1 | bytes 8 | tf_op jit(solution)/shard_map/while/body/eval_jaxpr/psum | solution.py:133
  905.3 11.0 %psum.33 = f32[]{:T(128)} all-reduce(f32[]{:T(128)} %bitcast.409), channel_id=1, replica_groups=mesh['gx'=4,'gy'=2,'gz'=4] {'gx'}, use_global_device_ids=true, to_apply=%region_17.17 | all-reduce | flops 1 | bytes 8 | tf_op jit(solution)/shard_map/while/body/eval_jaxpr/psum | solution.py:133
  917.5 12.4 %psum.32 = f32[1]{0:T(128)} all-reduce(f32[1]{0:T(128)} %bitcast.408), channel_id=1, replica_groups=mesh['gx'=4,'gy'=2,'gz'=4] {'gy','gz'}, use_global_device_ids=true, to_apply=%region_16.16 | all-reduce | flops 1 | bytes 8 | tf_op jit(solution)/shard_map/while/body/eval_jaxpr/psum | solution.py:133
  929.9 9.0 psum.33
  940.1 12.4 %psum.32 = f32[1]{0:T(128)} all-reduce(f32[1]{0:T(128)} %bitcast.408), channel_id=1, replica_groups=mesh['gx'=4,'gy'=2,'gz'=4] {'gy','gz'}, use_global_device_ids=true, to_apply=%region_16.16 | all-reduce | flops 1 | bytes 8 | tf_op jit(solution)/shard_map/while/body/eval_jaxpr/psum | solution.py:133
  952.5 11.0 %psum.33 = f32[]{:T(128)} all-reduce(f32[]{:T(128)} %bitcast.409), channel_id=1, replica_groups=mesh['gx'=4,'gy'=2,'gz'=4] {'gx'}, use_global_device_ids=true, to_apply=%region_17.17 | all-reduce | flops 1 | bytes 8 | tf_op jit(solution)/shard_map/while/body/eval_jaxpr/psum | solution.py:133
  964.7 12.4 %psum.32 = f32[1]{0:T(128)} all-reduce(f32[1]{0:T(128)} %bitcast.408), channel_id=1, replica_groups=mesh['gx'=4,'gy'=2,'gz'=4] {'gy','gz'}, use_global_device_ids=true, to_apply=%region_16.16 | all-reduce | flops 1 | bytes 8 | tf_op jit(solution)/shard_map/while/body/eval_jaxpr/psum | solution.py:133
  (715 shorter events, 714.2 us)
Async XLA Ops:
  47.5 18.1 %collective-permute-start.10 = (f32[1,18,10,1]{3,0,2,1:T(1,128)S(1)}, f32[1,18,10,1]{3,0,2,1:T(1,128)S(1)}, u32[]{:S(2)}, u32[]{:S(2)}) collective-permute-start(f32[1,18,10,1]{3,0,2,1:T(1,128)S(1)} %get-tuple-element.139), channel_id=1, source_target_pairs={{1,0},{2,1},{3,2},{5,4},{6,5},{7,6},{9,8},{10,9},{11,10},{13,12},{... | collective-permute-start | bytes 2168 | tf_op jit(solution)/shard_map/ppermute | solution.py:31
  48.8 16.8 %collective-permute-start.11 = (f32[1,18,10,1]{3,0,2,1:T(1,128)S(1)}, f32[1,18,10,1]{3,0,2,1:T(1,128)S(1)}, u32[]{:S(2)}, u32[]{:S(2)}) collective-permute-start(f32[1,18,10,1]{3,0,2,1:T(1,128)S(1)} %get-tuple-element.140), channel_id=1, source_target_pairs={{0,1},{1,2},{2,3},{4,5},{5,6},{6,7},{8,9},{9,10},{10,11},{12,13},{... | collective-permute-start | bytes 2168 | tf_op jit(solution)/shard_map/ppermute | solution.py:29
  126.7 12.0 %collective-permute-start.24 = (f32[1,1,2,64]{3,1,2,0:T(1,128)S(1)}, f32[1,1,2,64]{3,1,2,0:T(1,128)S(1)}, u32[]{:S(2)}, u32[]{:S(2)}) collective-permute-start(f32[1,1,2,64]{3,1,2,0:T(1,128)S(1)} %get-tuple-element.344), channel_id=1, source_target_pairs={{8,0},{16,8},{24,16},{9,1},{17,9},{25,17},{10,2},{18,10},{26,18},{... | collective-permute-start | bytes 1544 | tf_op jit(solution)/shard_map/ppermute | solution.py:31
  179.4 12.2 %collective-permute-start.36 = (f32[1,1,4,128]{3,2,1,0:T(4,128)S(1)}, f32[1,1,4,128]{3,2,1,0:T(4,128)S(1)}, u32[]{:S(2)}, u32[]{:S(2)}) collective-permute-start(f32[1,1,4,128]{3,2,1,0:T(4,128)S(1)} %get-tuple-element.282), channel_id=1, source_target_pairs={{8,0},{16,8},{24,16},{9,1},{17,9},{25,17},{10,2},{18,10},{26,18},{... | collective-permute-start | bytes 6152 | tf_op jit(solution)/shard_map/ppermute | solution.py:31
  198.9 18.4 %collective-permute-start.40 = (f32[1,10,6,1]{3,0,2,1:T(1,128)S(1)}, f32[1,10,6,1]{3,0,2,1:T(1,128)S(1)}, u32[]{:S(2)}, u32[]{:S(2)}) collective-permute-start(f32[1,10,6,1]{3,0,2,1:T(1,128)S(1)} %get-tuple-element.229), channel_id=1, source_target_pairs={{1,0},{2,1},{3,2},{5,4},{6,5},{7,6},{9,8},{10,9},{11,10},{13,12},{... | collective-permute-start | bytes 728 | tf_op jit(solution)/shard_map/ppermute | solution.py:31
  200.2 17.1 %collective-permute-start.41 = (f32[1,10,6,1]{3,0,2,1:T(1,128)S(1)}, f32[1,10,6,1]{3,0,2,1:T(1,128)S(1)}, u32[]{:S(2)}, u32[]{:S(2)}) collective-permute-start(f32[1,10,6,1]{3,0,2,1:T(1,128)S(1)} %get-tuple-element.230), channel_id=1, source_target_pairs={{0,1},{1,2},{2,3},{4,5},{5,6},{6,7},{8,9},{9,10},{10,11},{12,13},{... | collective-permute-start | bytes 728 | tf_op jit(solution)/shard_map/ppermute | solution.py:29
  326.5 12.0 %collective-permute-start.42 = (f32[1,1,8,256]{3,2,1,0:T(8,128)S(1)}, f32[1,1,8,256]{3,2,1,0:T(8,128)S(1)}, u32[]{:S(2)}, u32[]{:S(2)}) collective-permute-start(f32[1,1,8,256]{3,2,1,0:T(8,128)S(1)} %get-tuple-element.198), channel_id=1, source_target_pairs={{8,0},{16,8},{24,16},{9,1},{17,9},{25,17},{10,2},{18,10},{26,18},{... | collective-permute-start | bytes 24584 | tf_op jit(solution)/shard_map/ppermute | solution.py:31
  357.2 14.3 %collective-permute-start.48 = (f32[1,1,8,256]{3,2,1,0:T(8,128)S(1)}, f32[1,1,8,256]{3,2,1,0:T(8,128)S(1)}, u32[]{:S(2)}, u32[]{:S(2)}) collective-permute-start(f32[1,1,8,256]{3,2,1,0:T(8,128)S(1)} %get-tuple-element.196), channel_id=1, source_target_pairs={{8,0},{16,8},{24,16},{9,1},{17,9},{25,17},{10,2},{18,10},{26,18},{... | collective-permute-start | bytes 24584 | tf_op jit(solution)/shard_map/ppermute | solution.py:31
  358.5 13.0 %collective-permute-start.49 = (f32[1,1,8,256]{3,2,1,0:T(8,128)S(1)}, f32[1,1,8,256]{3,2,1,0:T(8,128)S(1)}, u32[]{:S(2)}, u32[]{:S(2)}) collective-permute-start(f32[1,1,8,256]{3,2,1,0:T(8,128)S(1)} %get-tuple-element.195), channel_id=1, source_target_pairs={{0,8},{8,16},{16,24},{1,9},{9,17},{17,25},{2,10},{10,18},{18,26},{... | collective-permute-start | bytes 24584 | tf_op jit(solution)/shard_map/ppermute | solution.py:29
  363.5 13.9 %collective-permute-start.136 = (f32[1,18,10,1]{3,0,2,1:T(1,128)S(1)}, f32[1,18,10,1]{3,0,2,1:T(1,128)S(1)}, u32[]{:S(2)}, u32[]{:S(2)}) collective-permute-start(f32[1,18,10,1]{3,0,2,1:T(1,128)S(1)} %get-tuple-element.155), channel_id=1, source_target_pairs={{1,0},{2,1},{3,2},{5,4},{6,5},{7,6},{9,8},{10,9},{11,10},{13,12},{... | collective-permute-start | bytes 2168 | tf_op jit(solution)/shard_map/ppermute | solution.py:31
  364.8 12.6 %collective-permute-start.137 = (f32[1,18,10,1]{3,0,2,1:T(1,128)S(1)}, f32[1,18,10,1]{3,0,2,1:T(1,128)S(1)}, u32[]{:S(2)}, u32[]{:S(2)}) collective-permute-start(f32[1,18,10,1]{3,0,2,1:T(1,128)S(1)} %get-tuple-element.156), channel_id=1, source_target_pairs={{0,1},{1,2},{2,3},{4,5},{5,6},{6,7},{8,9},{9,10},{10,11},{12,13},{... | collective-permute-start | bytes 2168 | tf_op jit(solution)/shard_map/ppermute | solution.py:29
  413.5 23.6 %collective-permute-start.141 = (f32[1,18,1,256]{3,2,1,0:T(1,128)S(1)}, f32[1,18,1,256]{3,2,1,0:T(1,128)S(1)}, u32[]{:S(2)}, u32[]{:S(2)}) collective-permute-start(f32[1,18,1,256]{3,2,1,0:T(1,128)S(1)} %get-tuple-element.176), channel_id=1, source_target_pairs={{0,4},{1,5},{2,6},{3,7},{8,12},{9,13},{10,14},{11,15},{16,20},{17,... | collective-permute-start | bytes 55304 | tf_op jit(solution)/shard_map/ppermute | solution.py:29
  415.3 21.8 %collective-permute-start.140 = (f32[1,18,1,256]{3,2,1,0:T(1,128)S(1)}, f32[1,18,1,256]{3,2,1,0:T(1,128)S(1)}, u32[]{:S(2)}, u32[]{:S(2)}) collective-permute-start(f32[1,18,1,256]{3,2,1,0:T(1,128)S(1)} %get-tuple-element.175), channel_id=1, source_target_pairs={{4,0},{5,1},{6,2},{7,3},{12,8},{13,9},{14,10},{15,11},{20,16},{21,... | collective-permute-start | bytes 55304 | tf_op jit(solution)/shard_map/ppermute | solution.py:31
  445.7 12.6 %collective-permute-start.64 = (f32[1,10,6,1]{3,0,2,1:T(1,128)S(1)}, f32[1,10,6,1]{3,0,2,1:T(1,128)S(1)}, u32[]{:S(2)}, u32[]{:S(2)}) collective-permute-start(f32[1,10,6,1]{3,0,2,1:T(1,128)S(1)} %get-tuple-element.225), channel_id=1, source_target_pairs={{1,0},{2,1},{3,2},{5,4},{6,5},{7,6},{9,8},{10,9},{11,10},{13,12},{... | collective-permute-start | bytes 728 | tf_op jit(solution)/shard_map/ppermute | solution.py:31
  451.4 14.5 %collective-permute-start.142 = (f32[1,18,10,1]{3,0,2,1:T(1,128)S(1)}, f32[1,18,10,1]{3,0,2,1:T(1,128)S(1)}, u32[]{:S(2)}, u32[]{:S(2)}) collective-permute-start(f32[1,18,10,1]{3,0,2,1:T(1,128)S(1)} %get-tuple-element.151), channel_id=1, source_target_pairs={{1,0},{2,1},{3,2},{5,4},{6,5},{7,6},{9,8},{10,9},{11,10},{13,12},{... | collective-permute-start | bytes 2168 | tf_op jit(solution)/shard_map/ppermute | solution.py:31
  452.7 13.2 %collective-permute-start.143 = (f32[1,18,10,1]{3,0,2,1:T(1,128)S(1)}, f32[1,18,10,1]{3,0,2,1:T(1,128)S(1)}, u32[]{:S(2)}, u32[]{:S(2)}) collective-permute-start(f32[1,18,10,1]{3,0,2,1:T(1,128)S(1)} %get-tuple-element.152), channel_id=1, source_target_pairs={{0,1},{1,2},{2,3},{4,5},{5,6},{6,7},{8,9},{9,10},{10,11},{12,13},{... | collective-permute-start | bytes 2168 | tf_op jit(solution)/shard_map/ppermute | solution.py:29
  480.8 12.0 %collective-permute-start.72 = (f32[1,1,2,64]{3,1,2,0:T(1,128)S(1)}, f32[1,1,2,64]{3,1,2,0:T(1,128)S(1)}, u32[]{:S(2)}, u32[]{:S(2)}) collective-permute-start(f32[1,1,2,64]{3,1,2,0:T(1,128)S(1)} %get-tuple-element.338), channel_id=1, source_target_pairs={{8,0},{16,8},{24,16},{9,1},{17,9},{25,17},{10,2},{18,10},{26,18},{... | collective-permute-start | bytes 1544 | tf_op jit(solution)/shard_map/ppermute | solution.py:31
  533.4 12.2 %collective-permute-start.84 = (f32[1,1,4,128]{3,2,1,0:T(4,128)S(1)}, f32[1,1,4,128]{3,2,1,0:T(4,128)S(1)}, u32[]{:S(2)}, u32[]{:S(2)}) collective-permute-start(f32[1,1,4,128]{3,2,1,0:T(4,128)S(1)} %get-tuple-element.270), channel_id=1, source_target_pairs={{8,0},{16,8},{24,16},{9,1},{17,9},{25,17},{10,2},{18,10},{26,18},{... | collective-permute-start | bytes 6152 | tf_op jit(solution)/shard_map/ppermute | solution.py:31
  553.0 18.3 %collective-permute-start.88 = (f32[1,10,6,1]{3,0,2,1:T(1,128)S(1)}, f32[1,10,6,1]{3,0,2,1:T(1,128)S(1)}, u32[]{:S(2)}, u32[]{:S(2)}) collective-permute-start(f32[1,10,6,1]{3,0,2,1:T(1,128)S(1)} %get-tuple-element.221), channel_id=1, source_target_pairs={{1,0},{2,1},{3,2},{5,4},{6,5},{7,6},{9,8},{10,9},{11,10},{13,12},{... | collective-permute-start | bytes 728 | tf_op jit(solution)/shard_map/ppermute | solution.py:31
  554.3 17.1 %collective-permute-start.89 = (f32[1,10,6,1]{3,0,2,1:T(1,128)S(1)}, f32[1,10,6,1]{3,0,2,1:T(1,128)S(1)}, u32[]{:S(2)}, u32[]{:S(2)}) collective-permute-start(f32[1,10,6,1]{3,0,2,1:T(1,128)S(1)} %get-tuple-element.222), channel_id=1, source_target_pairs={{0,1},{1,2},{2,3},{4,5},{5,6},{6,7},{8,9},{9,10},{10,11},{12,13},{... | collective-permute-start | bytes 728 | tf_op jit(solution)/shard_map/ppermute | solution.py:29
  644.8 12.0 %collective-permute-start.170 = (f32[1,6,1,64]{3,1,2,0:T(8,128)S(1)}, f32[1,6,1,64]{3,1,2,0:T(8,128)S(1)}, u32[]{:S(2)}, u32[]{:S(2)}) collective-permute-start(f32[1,6,1,64]{3,1,2,0:T(8,128)S(1)} %get-tuple-element.324), channel_id=1, source_target_pairs={{4,0},{5,1},{6,2},{7,3},{12,8},{13,9},{14,10},{15,11},{20,16},{21,... | collective-permute-start | bytes 4616 | tf_op jit(solution)/shard_map/ppermute | solution.py:31
  650.7 19.5 %collective-permute-start.90 = (f32[1,1,8,256]{3,2,1,0:T(8,128)S(1)}, f32[1,1,8,256]{3,2,1,0:T(8,128)S(1)}, u32[]{:S(2)}, u32[]{:S(2)}) collective-permute-start(f32[1,1,8,256]{3,2,1,0:T(8,128)S(1)} %get-tuple-element.192), channel_id=1, source_target_pairs={{8,0},{16,8},{24,16},{9,1},{17,9},{25,17},{10,2},{18,10},{26,18},{... | collective-permute-start | bytes 24584 | tf_op jit(solution)/shard_map/ppermute | solution.py:31
  652.0 18.2 %collective-permute-start.91 = (f32[1,1,8,256]{3,2,1,0:T(8,128)S(1)}, f32[1,1,8,256]{3,2,1,0:T(8,128)S(1)}, u32[]{:S(2)}, u32[]{:S(2)}) collective-permute-start(f32[1,1,8,256]{3,2,1,0:T(8,128)S(1)} %get-tuple-element.191), channel_id=1, source_target_pairs={{0,8},{8,16},{16,24},{1,9},{9,17},{17,25},{2,10},{10,18},{18,26},{... | collective-permute-start | bytes 24584 | tf_op jit(solution)/shard_map/ppermute | solution.py:29
  683.2 13.1 %collective-permute-start.92 = (f32[1,18,1,256]{3,2,1,0:T(1,128)S(1)}, f32[1,18,1,256]{3,2,1,0:T(1,128)S(1)}, u32[]{:S(2)}, u32[]{:S(2)}) collective-permute-start(f32[1,18,1,256]{3,2,1,0:T(1,128)S(1)} %get-tuple-element.162), channel_id=1, source_target_pairs={{4,0},{5,1},{6,2},{7,3},{12,8},{13,9},{14,10},{15,11},{20,16},{21,... | collective-permute-start | bytes 55304 | tf_op jit(solution)/shard_map/ppermute | solution.py:31
  (169 other events, 1256.3 us)
